TPU v7x, 128 devices: a whole 4x4x4 slice. The times are simulated.
128 devices in a mesh: gx: 4 (over z), gy: 4 (over y_lo, core), gz: 8 (over y_hi, x).
Axes of the slice: x: 4, y: 4 (y_hi: 2, y_lo: 2; y = y_hi * 2 + y_lo), z: 4, core: 2. Of those that a mesh axis runs over, the one named last changes fastest.
Arguments:
- tokens: bfloat16 [2048, 18432], P(('gx', 'gy'), 'gz'), may hold values from -6 to 6
- up_weight: bfloat16 [18432, 36864], P('gz', ('gx', 'gy')), may hold values from -0.046875 to 0.046875
- down_weight: bfloat16 [36864, 18432], P(('gx', 'gy'), 'gz'), may hold values from -0.03125 to 0.03125
- readout: bfloat16 [18432], P('gz'), may hold values from -0.046875 to 0.046875
- segment_ids: int32 [2048], replicated, may hold values from 0 to 7, never falling along the last dimension, each value on 1 to 512 neighbouring positions
Outputs:
- mixed_out: bfloat16 [2048, 18432], P(('gx', 'gy'), 'gz')
- seq_scores: float32 [8], replicated
Inputs may be any that keep to these rules, and one draw needn't show every extreme that they name: `segment_ids`: segment numbers never fall along the tokens; each of the 8 sequences holds 1 to 512 tokens, and one holds exactly 512.
All inputs are finite; a program needn't handle non-finite values.
Results may differ from a plain program's by a relative error of at most 0.0044.
Values may be sent and summed in bfloat16 or wider, within the bound.
A program may use at most 128 MiB of HBM per device.

v0:
```python
import jax
import jax.numpy as jnp
from jax import lax
from jax.sharding import PartitionSpec as P

SEGS = 8


def squared(values):
    return jnp.square(jnp.maximum(values, 0.0)).astype(jnp.bfloat16)


def per_device(tokens, up_weight, down_weight, readout, segment_ids):
    tok_rows = tokens.shape[0]
    gathered = lax.all_gather(tokens, ("gx", "gy"), axis=0, tiled=True)
    picked = gathered
    shares = lax.psum_scatter(
        jnp.dot(picked, up_weight, preferred_element_type=jnp.float32),
        "gz",
        scatter_dimension=0,
        tiled=True,
    )
    activated = lax.all_gather(squared(shares), "gz", axis=0, tiled=True)
    picked = activated
    branch = lax.psum_scatter(
        jnp.dot(picked, down_weight, preferred_element_type=jnp.float32),
        ("gx", "gy"),
        scatter_dimension=0,
        tiled=True,
    )
    combined = tokens.astype(jnp.float32) + branch
    mixed_out = combined.astype(jnp.bfloat16)
    labels = jnp.arange(SEGS, dtype=jnp.int32)
    offset = lax.axis_index(("gx", "gy")) * tok_rows
    own_ids = lax.dynamic_slice_in_dim(segment_ids, offset, tok_rows, 0)
    own_hot = (own_ids[:, None] == labels[None, :]).astype(jnp.float32)
    all_hot = (segment_ids[:, None] == labels[None, :]).astype(jnp.float32)
    weights_read = readout.astype(jnp.float32)
    token_score = jnp.sum(combined * weights_read[None, :], axis=1)
    partial_total = jnp.sum(own_hot * token_score[:, None], axis=0)
    segment_total = lax.psum(partial_total, ("gx", "gy", "gz"))
    counts = jnp.sum(all_hot, axis=0)
    return (mixed_out, segment_total / jnp.sqrt(counts))


def solution(mesh):
    placed = (P(("gx", "gy"), "gz"), P("gz", ("gx", "gy")), P(("gx", "gy"), "gz"), P("gz"), P())
    return jax.shard_map(
        per_device,
        mesh=mesh,
        in_specs=placed,
        out_specs=(P(("gx", "gy"), "gz"), P()),
        check_vma=False,
    )
```

profile of v0, /device:TPU:1, one launch (start us, length us, event | category | flops | bytes accessed | tf_op | source)
XLA Modules:
  0.0 739.0 jit_solution(13112862827725781808)
XLA Ops:
  7.2 0.0 all-gather.3.cloned.1.call-start
  7.2 0.7 all-gather.3.cloned.1.call-update
  7.9 0.0 reduce-scatter.3.cloned.1.call-start
  7.9 62.5 %all-gather.3.cloned.1.call-done = bf16[2048,2304]{1,0:T(8,128)(2,1)} async-done(((bf16[128,2304]{1,0:T(8,128)(2,1)}), bf16[2048,2304]{1,0:T(8,128)(2,1)}) %all-gather.3.cloned.1.call-update) | async-done | bytes 9437200 | tf_op jit(solution)/shard_map/all_gather | solution.py:15
  70.5 30.2 %fusion.1 = f32[2048,2304]{1,0:T(8,128)} fusion(bf16[2048,2304]{1,0:T(8,128)(2,1)} %all-gather.3.cloned.1.call-done, bf16[2304,2304]{1,0:T(8,128)(2,1)} %param.6), kind=kOutput, calls=%fused_computation.9 | convolution fusion | flops 21743271936 | bytes 38928384 | tf_op jit(solution)/shard_map/dot_general | solution.py:18
  100.6 0.0 reduce-scatter.3.cloned.1.call-update
  100.7 0.0 all-gather.5.cloned.1.call-start
  100.7 209.4 %reduce-scatter.3.cloned.1.call-done = f32[256,2304]{1,0:T(8,128)} async-done(((f32[2048,2304]{1,0:T(8,128)}), f32[256,2304]{1,0:T(8,128)}) %reduce-scatter.3.cloned.1.call-update) | async-done | bytes 2359312 | tf_op jit(solution)/shard_map/reduce_scatter | solution.py:17
  310.1 2.9 multiply_convert_fusion
  312.9 0.0 all-gather.5.cloned.1.call-update
  313.0 0.2 reduce-scatter.5.cloned.1.call-start
  313.2 120.0 %all-gather.5.cloned.1.call-done = bf16[2048,2304]{1,0:T(8,128)(2,1)} async-done(((bf16[256,2304]{1,0:T(8,128)(2,1)}), bf16[2048,2304]{1,0:T(8,128)(2,1)}) %all-gather.5.cloned.1.call-update) | async-done | bytes 9437200 | tf_op jit(solution)/shard_map/all_gather | solution.py:23
  433.2 30.2 %fusion.2 = f32[2048,2304]{1,0:T(8,128)} fusion(bf16[2048,2304]{1,0:T(8,128)(2,1)} %all-gather.5.cloned.1.call-done, bf16[2304,2304]{1,0:T(8,128)(2,1)} %param.7), kind=kOutput, calls=%fused_computation.10 | convolution fusion | flops 21743271936 | bytes 38928384 | tf_op jit(solution)/shard_map/dot_general | solution.py:26
  463.4 0.0 copy-start.2
  463.4 0.0 copy-start.1
  463.4 0.0 copy-start
  463.4 0.0 reduce-scatter.5.cloned.1.call-update
  463.4 0.7 copy-done.2
  464.1 0.0 copy-done.1
  464.1 0.1 dynamic_slice.3
  464.2 199.6 %reduce-scatter.5.cloned.1.call-done = f32[128,2304]{1,0:T(8,128)} async-done(((f32[2048,2304]{1,0:T(8,128)}), f32[128,2304]{1,0:T(8,128)}) %reduce-scatter.5.cloned.1.call-update) | async-done | bytes 1179664 | tf_op jit(solution)/shard_map/reduce_scatter | solution.py:25
  663.7 0.0 copy-done
  663.8 2.3 multiply_reduce_fusion
  666.0 0.1 select_reduce_fusion
  666.2 0.1 convert_reduce_fusion
  666.3 65.6 %psum.7 = f32[8]{0:T(128)S(1)} all-reduce(f32[8]{0:T(128)S(1)} %select_reduce_fusion), channel_id=1, replica_groups=mesh['gx'=4,'gy'=4,'gz'=8] {'gx','gy','gz'}, use_global_device_ids=true, to_apply=%region_4.0 | all-reduce | flops 8 | bytes 64 | tf_op jit(solution)/shard_map/psum | solution.py:41
  731.9 0.5 rsqrt_multiply_fusion
  (1 shorter events, 0.0 us)
Async XLA Ops:
  7.2 63.3 %all-gather.3.cloned.1.call-start = ((), (), s32[]{:S(2)}) async-start(), calls=%async_computation.2 | async-start | bytes 10027008 | tf_op jit(solution)/shard_map/all_gather | solution.py:15
  7.9 302.2 %reduce-scatter.3.cloned.1.call-start = ((), (), s32[]{:S(2)}) async-start(), calls=%async_computation.3 | async-start | bytes 21233664 | tf_op jit(solution)/shard_map/reduce_scatter | solution.py:17
  100.7 332.6 %all-gather.5.cloned.1.call-start = ((), (), s32[]{:S(2)}) async-start(), calls=%async_computation.4 | async-start | bytes 10616832 | tf_op jit(solution)/shard_map/all_gather | solution.py:23
  313.0 350.8 %reduce-scatter.5.cloned.1.call-start = ((), (), s32[]{:S(2)}) async-start(), calls=%async_computation.5 | async-start | bytes 20054016 | tf_op jit(solution)/shard_map/reduce_scatter | solution.py:25
  463.4 0.7 copy-start.2
  463.4 0.7 copy-start.1
  463.4 200.3 %copy-start = (bf16[128,2304]{1,0:T(8,128)(2,1)S(1)}, bf16[128,2304]{1,0:T(8,128)(2,1)}, u32[]{:S(2)}) copy-start(bf16[128,2304]{1,0:T(8,128)(2,1)} %param.5) | copy-start | bytes 1769476
Sparse Core Ops, SparseCore 0:
  9.7 60.7 all-gather.2
  100.8 209.2 reduce-scatter.2
  313.1 120.1 all-gather.4
  463.6 200.1 reduce-scatter.4
where the time goes:
time: 739 us
  waiting for transfers between devices  592 us (80%)
  blocking collectives  65.6 us (9%)
  matrix products  60.3 us (8%)
  between operations  13.8 us (2%)
    reduce_scatter x1, waiting for transfers between devices, per_device(): lax.psum_scatter(jnp.dot(picked, up_weight, preferred_element_type=jnp.fl...  209 us
    reduce_scatter x1, waiting for transfers between devices, per_device(): lax.psum_scatter(jnp.dot(picked, down_weight, preferred_element_type=jnp....  200 us
    all_gather x1, waiting for transfers between devices, per_device(): activated = lax.all_gather(squared(shares), 'gz', axis=0, tiled=True)  120 us
    psum x1, blocking collectives, per_device(): segment_total = lax.psum(partial_total, ('gx', 'gy', 'gz'))  65.6 us
    all_gather x1, waiting for transfers between devices, per_device(): gathered = lax.all_gather(tokens, ('gx', 'gy'), axis=0, tiled=True)  62.5 us
    dot_general x1, matrix products, per_device(): jnp.dot(picked, up_weight, preferred_element_type=jnp.float32)  30.2 us
    dot_general x1, matrix products, per_device(): jnp.dot(picked, down_weight, preferred_element_type=jnp.float32)  30.2 us
  transfers between devices with their start and end apart: 4, of which 4 were waited for; matrix products, arithmetic and copies ran while one was open for 0% of the time, Pallas kernels for 0%

commit v1 on v0

v1 whole, which is shorter than its diff:
```python
import functools

import jax
import jax.numpy as jnp
from jax import lax
from jax.experimental import pallas as pl
from jax.experimental.pallas import tpu as pltpu
from jax.sharding import PartitionSpec as P

MESH = pl.DeviceIdType.MESH
SEGS = 8
PIECES = 16
CHUNK = 16
TILE = 256
PAIR_Z = (0, 1, 3, 2, 1, 3, 2, 0)
PAIR_L = (0, 0, 0, 0, 1, 1, 1, 1)
STAGES = (("own", 7), ("up", 0), ("pass", 1), ("sum", 2), ("act", 3), ("fwd", 4), ("back", 5), ("down", 6))
LAST = max(lag for _, lag in STAGES)
PART_RING = 3


def packed(table, bits):
    return sum(v << (bits * k) for k, v in enumerate(table))


def lookup(table, bits, k):
    return (packed(table, bits) >> (bits * k)) % (1 << bits)


def kernel(
    tok_hbm, up_hbm, down_hbm, read_ref, own_ids_ref, ids_ref, out_ref, score_ref,
    wu, wd, tk, pf, s1s, s2s, s1r, s2r, s3s, keep, s3r, mo, acc, xs, xr, p4s, p4r, ar1, ar2,
    w_sem, tok_sem, p1_s, p1_r, fw_s, s1_s, s1_r, s2_s, s2_r, s3_s, s3_r, s4_s, s4_r, s5_s, s5_r, s6_s, s6_r,
    x_s, x_r, p4_s, p4_r, ar1_s, ar1_r, ar2_s, ar2_r,
):
    z = lax.axis_index("gx")
    gy = lax.axis_index("gy")
    gz = lax.axis_index("gz")
    low, core = gy // 2, gy % 2
    high, x = gz // 4, gz % 4
    block = z * 4 + gy

    def in_group(gz_to):
        return (z, gy, gz_to)

    right = in_group(high * 4 + (x + 1) % 4)
    left = in_group(high * 4 + (x + 3) % 4)
    across = in_group((1 - high) * 4 + x)
    twin = (z, low * 2 + 1 - core, gz)

    def chunk(dx, j):
        at = ((x + dx) % 4) * 2 + (high + j) % 2
        return pl.ds(pl.multiple_of(at * CHUNK, CHUNK), CHUNK)

    def rcopy(src, dst, ss, rs, to):
        return pltpu.make_async_remote_copy(
            src_ref=src, dst_ref=dst, send_sem=ss, recv_sem=rs, device_id=to, device_id_type=MESH
        )

    barrier = pltpu.get_barrier_semaphore()
    for d in range(1, 8):
        pl.semaphore_signal(barrier, inc=1, device_id=in_group((gz + d) % 8), device_id_type=MESH)
    for d in range(1, 16):
        to = (block + d) % 16
        pl.semaphore_signal(barrier, inc=1, device_id=(to // 4, to % 4, gz), device_id_type=MESH)

    load_tok = pltpu.make_async_copy(tok_hbm, tk.at[0], tok_sem)
    load_up = pltpu.make_async_copy(up_hbm, wu, w_sem.at[0])
    load_down = pltpu.make_async_copy(down_hbm, wd, w_sem.at[1])
    load_tok.start()
    load_up.start()
    load_down.start()
    pl.semaphore_wait(barrier, 22)

    def gather(k):
        dz, dl = lookup(PAIR_Z, 2, k), lookup(PAIR_L, 1, k)
        to = ((z + 4 - dz) % 4, ((low + dl) % 2) * 2 + core, gz)
        return rcopy(tok_hbm, tk.at[2 * k - 1], p1_s.at[k], p1_r.at[2 * k - 1], to)

    to_twin = rcopy(tok_hbm, tk.at[15], p1_s.at[0], p1_r.at[15], twin)
    gather(1).start()
    gather(2).start()
    to_twin.start()
    load_tok.wait()
    load_up.wait()

    def forward(i):
        return rcopy(tk.at[i], tk.at[i + 1], fw_s, p1_r.at[i + 1], twin)

    def first(i, n):
        q = i % 2
        if n < 2:
            return rcopy(s1s.at[q, n], s1r.at[i, n], s1_s.at[n, q], s1_r.at[n, i], (right, left)[n])
        return rcopy(s1s.at[q, n], s2r.at[i, n - 2], s1_s.at[n, q], s2_r.at[n - 2, i], (right, left)[n - 2])

    def second(i, n):
        q = i % 2
        return rcopy(s2s.at[q, n], s2r.at[i, n + 2], s2_s.at[n, q], s2_r.at[n + 2, i], (right, left)[n])

    def third(i):
        q = i % 2
        return rcopy(s3s.at[q], s3r.at[i], s3_s.at[q], s3_r.at[i], across)

    def spread(i, dx, j, ss, rs, to):
        place = tk.at[i, chunk(dx, j)]
        return rcopy(place, place, ss, rs, to)

    def fourth(i):
        return spread(i, 0, 0, s4_s.at[i], s4_r.at[i], across)

    def fifth(i, j, n):
        return spread(i, 0, j, s5_s.at[2 * j + n, i], s5_r.at[2 * j + n, i], (right, left)[n])

    def fifth_in(i, j, n):
        return spread(i, (3, 1)[n], j, s5_s.at[2 * j + n, i], s5_r.at[2 * j + n, i], (right, left)[n])

    def sixth(i, n):
        return spread(i, (3, 1)[n], n, s6_s.at[n, i], s6_r.at[n, i], (right, left)[n])

    def sixth_in(i, n):
        return spread(i, 2, n, s6_s.at[n, i], s6_r.at[n, i], (right, left)[n])

    def exchange(k):
        return rcopy(xs, xr.at[k % 2], x_s, x_r.at[k], twin)

    def owner(k):
        dz, dl = lookup(PAIR_Z, 2, k), lookup(PAIR_L, 1, k)
        to = ((z + dz) % 4, ((low + dl) % 2) * 2 + core, gz)
        return rcopy(p4s.at[k % 2], p4r.at[k - 1], p4_s.at[k % 2], p4_r.at[k - 1], to)

    def up(i):
        @pl.when(i > 0)
        def _():
            rcopy(tk.at[i], tk.at[i], p1_s.at[0], p1_r.at[i], twin).wait_recv()

        passes = (i % 2 == 1) & (i < PIECES - 1)

        @pl.when(passes)
        def _():
            forward(i).start()

        p = i % PART_RING

        @pl.loop(0, wu.shape[1] // TILE)
        def _(n):
            cols = pl.ds(pl.multiple_of(n * TILE, TILE), TILE)
            pf[p, :, cols] = jnp.dot(tk[i], wu[:, cols], preferred_element_type=jnp.float32)

        @pl.when(i >= 2)
        def _():
            for n in range(4):
                first(i - 2, n).wait_send()

        @pl.when(passes)
        def _():
            forward(i).wait_send()

        q = i % 2
        s1s[q, 0] = pf[p, chunk(2, 0)].astype(jnp.bfloat16)
        s1s[q, 1] = pf[p, chunk(2, 1)].astype(jnp.bfloat16)
        first(i, 0).start()
        first(i, 1).start()
        s1s[q, 2] = pf[p, chunk(1, 1)].astype(jnp.bfloat16)
        s1s[q, 3] = pf[p, chunk(3, 0)].astype(jnp.bfloat16)
        first(i, 2).start()
        first(i, 3).start()

    def pass_on(i):
        p, q = i % PART_RING, i % 2

        @pl.when(i >= 2)
        def _():
            second(i - 2, 0).wait_send()
            second(i - 2, 1).wait_send()

        first(i, 0).wait_recv()
        s2s[q, 0] = (pf[p, chunk(1, 0)] + s1r[i, 0].astype(jnp.float32)).astype(jnp.bfloat16)
        second(i, 0).start()
        first(i, 1).wait_recv()
        s2s[q, 1] = (pf[p, chunk(3, 1)] + s1r[i, 1].astype(jnp.float32)).astype(jnp.bfloat16)
        second(i, 1).start()

    def sum_up(i):
        p, q = i % PART_RING, i % 2

        @pl.when(i >= 2)
        def _():
            third(i - 2).wait_send()

        first(i, 2).wait_recv()
        second(i, 1).wait_recv()
        s3s[q] = (
            pf[p, chunk(0, 1)] + s2r[i, 0].astype(jnp.float32) + s2r[i, 3].astype(jnp.float32)
        ).astype(jnp.bfloat16)
        third(i).start()
        first(i, 3).wait_recv()
        second(i, 0).wait_recv()
        keep[q] = pf[p, chunk(0, 0)] + s2r[i, 1].astype(jnp.float32) + s2r[i, 2].astype(jnp.float32)

    def act(i):
        third(i).wait_recv()
        total = keep[i % 2] + s3r[i].astype(jnp.float32)
        tk[i, chunk(0, 0)] = jnp.square(jnp.maximum(total, 0.0)).astype(jnp.bfloat16)
        fifth(i, 0, 0).start()
        fifth(i, 0, 1).start()
        fourth(i).start()

    def fwd(i):
        spread(i, 0, 1, s4_s.at[i], s4_r.at[i], across).wait_recv()
        fifth(i, 1, 0).start()
        fifth(i, 1, 1).start()
        fifth_in(i, 0, 0).wait_recv()
        sixth(i, 0).start()

    def back(i):
        fifth_in(i, 1, 1).wait_recv()
        sixth(i, 1).start()

    def down(i):
        @pl.when(i == 0)
        def _():
            load_down.wait()

        fifth_in(i, 0, 1).wait_recv()
        fifth_in(i, 1, 0).wait_recv()
        sixth_in(i, 0).wait_recv()
        sixth_in(i, 1).wait_recv()
        k = (i + 1) // 2

        def product(store):
            @pl.loop(0, wd.shape[1] // TILE)
            def _(n):
                cols = pl.ds(pl.multiple_of(n * TILE, TILE), TILE)
                store(cols, jnp.dot(tk[i], wd[:, cols], preferred_element_type=jnp.float32))

        kept = (i % 2 == 1) & (i < PIECES - 1)

        @pl.when(kept | (i == 0))
        def _():
            def store(cols, value):
                mo[k % 3, :, cols] = value

            product(store)

        @pl.when(((i % 2 == 0) & (i > 0)) | (i == PIECES - 1))
        def _():
            @pl.when(k > 1)
            def _():
                exchange(k - 1).wait_send()

            def store(cols, value):
                xs[:, cols] = value

            product(store)
            exchange(k).start()

        @pl.when(i == 0)
        def _():
            acc[...] = mo[0] + out_ref[...].astype(jnp.float32)

    def own(i):
        k = i // 2

        @pl.when((i % 2 == 0) & (i > 0))
        def _():
            exchange(k).wait_recv()

            @pl.when(k > 2)
            def _():
                owner(k - 2).wait_send()

            p4s[k % 2] = (mo[k % 3] + xr[k % 2]).astype(jnp.bfloat16)
            owner(k).start()

        fourth(i).wait_send()
        for n in range(2):
            fifth(i, 0, n).wait_send()
            fifth(i, 1, n).wait_send()
            sixth(i, n).wait_send()

    work = dict(up=up, sum=sum_up, act=act, fwd=fwd, back=back, down=down, own=own)
    work["pass"] = pass_on
    out_ref[...] = tk[0]

    @pl.loop(0, PIECES + LAST)
    def _(t):
        k = t // 2 + 2

        @pl.when((t % 2 == 0) & (t > 0) & (k < 8))
        def _():
            gather(k).start()

        for name, lag in STAGES:
            @pl.when((t >= lag) & (t < lag + PIECES))
            def _(name=name, lag=lag):
                work[name](t - lag)

    for i in (PIECES - 2, PIECES - 1):
        for n in range(4):
            first(i, n).wait_send()
        second(i, 0).wait_send()
        second(i, 1).wait_send()
        third(i).wait_send()
    to_twin.wait_send()
    for k in range(1, 8):
        gather(k).wait_send()
    owner(6).wait_send()
    owner(7).wait_send()
    exchange(8).wait_send()

    for k in range(1, 8):
        owner(k).wait_recv()
    exchange(8).wait_recv()
    lanes = lax.broadcasted_iota(jnp.int32, (CHUNK, 128), 1)
    score_ref[...] = jnp.zeros_like(score_ref)

    @pl.loop(0, PIECES // 2)
    def _(r):
        rows = pl.ds(pl.multiple_of(r * CHUNK, CHUNK), CHUNK)
        total = acc[rows] + xr[0, rows]
        for k in range(7):
            total = total + p4r[k, rows].astype(jnp.float32)
        out_ref[rows] = total.astype(jnp.bfloat16)
        score = jnp.sum(total * read_ref[...].astype(jnp.float32), axis=1, keepdims=True)
        hot = own_ids_ref[rows] == lanes
        part = jnp.sum(jnp.where(hot, score, 0.0), axis=0, keepdims=True)
        score_ref[0:1] = score_ref[0:1] + part

    ar1[gz] = score_ref[...]
    sends = []
    for d in range(1, 8):
        sends.append(rcopy(ar1.at[gz], ar1.at[gz], ar1_s.at[d], ar1_r.at[d], in_group((gz + d) % 8)))
    for s in sends:
        s.start()
    for s in sends:
        s.wait()
    part = ar1[0]
    for d in range(1, 8):
        part = part + ar1[d]
    ar2[block] = part
    sends = []
    for d in range(1, 16):
        to = (block + d) % 16
        sends.append(rcopy(ar2.at[block], ar2.at[block], ar2_s.at[d], ar2_r.at[d], (to // 4, to % 4, gz)))
    for s in sends:
        s.start()
    for s in sends:
        s.wait()
    part = ar2[0]
    for d in range(1, 16):
        part = part + ar2[d]
    ids = ids_ref[...]
    lane = lax.broadcasted_iota(jnp.int32, (8, 128), 1)
    counts = jnp.ones((8, 128), jnp.float32)
    for s in range(SEGS):
        counts = jnp.where(lane == s, jnp.sum((ids == s).astype(jnp.float32)), counts)
    score_ref[...] = part / jnp.sqrt(counts)


def per_device(tokens, up_weight, down_weight, readout, segment_ids):
    rows, width = tokens.shape
    hidden = up_weight.shape[1]
    bf16, f32 = jnp.bfloat16, jnp.float32
    offset = lax.axis_index(("gx", "gy")) * rows
    own_ids = lax.dynamic_slice_in_dim(segment_ids, offset, rows, 0)
    own_ids = jnp.broadcast_to(own_ids[:, None], (rows, 128))
    ids = segment_ids.reshape(-1, 128)
    dma = pltpu.SemaphoreType.DMA
    vmem = pl.BlockSpec(memory_space=pltpu.VMEM)
    hbm = pl.BlockSpec(memory_space=pltpu.HBM)
    mixed, scores = pl.pallas_call(
        kernel,
        out_shape=(
            jax.ShapeDtypeStruct((rows, width), bf16),
            jax.ShapeDtypeStruct((8, 128), f32),
        ),
        in_specs=[hbm, hbm, hbm, vmem, vmem, vmem],
        out_specs=(vmem, vmem),
        scratch_shapes=[
            pltpu.VMEM(up_weight.shape, bf16),
            pltpu.VMEM(down_weight.shape, bf16),
            pltpu.VMEM((PIECES, rows, width), bf16),
            pltpu.VMEM((PART_RING, rows, hidden), f32),
            pltpu.VMEM((2, 4, CHUNK, hidden), bf16),
            pltpu.VMEM((2, 2, CHUNK, hidden), bf16),
            pltpu.VMEM((PIECES, 2, CHUNK, hidden), bf16),
            pltpu.VMEM((PIECES, 4, CHUNK, hidden), bf16),
            pltpu.VMEM((2, CHUNK, hidden), bf16),
            pltpu.VMEM((2, CHUNK, hidden), f32),
            pltpu.VMEM((PIECES, CHUNK, hidden), bf16),
            pltpu.VMEM((3, rows, width), f32),
            pltpu.VMEM((rows, width), f32),
            pltpu.VMEM((rows, width), f32),
            pltpu.VMEM((2, rows, width), f32),
            pltpu.VMEM((2, rows, width), bf16),
            pltpu.VMEM((7, rows, width), bf16),
            pltpu.VMEM((8, 8, 128), f32),
            pltpu.VMEM((16, 8, 128), f32),
            dma((2,)), dma, dma((8,)), dma((PIECES,)), dma,
            dma((4, 2)), dma((2, PIECES)),
            dma((2, 2)), dma((4, PIECES)),
            dma((2,)), dma((PIECES,)),
            dma((PIECES,)), dma((PIECES,)),
            dma((4, PIECES)), dma((4, PIECES)),
            dma((2, PIECES)), dma((2, PIECES)),
            dma, dma((9,)),
            dma((2,)), dma((7,)),
            dma((8,)), dma((8,)), dma((16,)), dma((16,)),
        ],
        compiler_params=pltpu.CompilerParams(
            collective_id=0, has_side_effects=True, vmem_limit_bytes=63 * 2**20
        ),
        cost_estimate=pl.CostEstimate(
            flops=4 * PIECES * rows * width * hidden, bytes_accessed=4 * width * hidden, transcendentals=0
        ),
        name="feed_forward",
    )(tokens, up_weight, down_weight, readout.reshape(1, -1), own_ids, ids)
    return mixed, scores[0, :SEGS]


def solution(mesh):
    placed = (P(("gx", "gy"), "gz"), P("gz", ("gx", "gy")), P(("gx", "gy"), "gz"), P("gz"), P())
    return jax.shard_map(
        per_device,
        mesh=mesh,
        in_specs=placed,
        out_specs=(P(("gx", "gy"), "gz"), P()),
        check_vma=False,
    )
```

time: 739 us -> 248 us (0.34)
  waiting for transfers between devices: 592 us -> 0 us
  Pallas kernels: 0 us -> 241 us
  blocking collectives: 65.6 us -> 0 us
  matrix products: 60.3 us -> 0 us
  between operations: 13.8 us -> 0.65 us
    reduce_scatter x2 -> x0, waiting for transfers between devices: 409 us -> none  [the longest x1 209 us: per_device(): lax.psum_scatter(jnp.dot(picked, up_weight, preferred_element_type=jnp.fl...]
    pallas_call x0 -> x1, Pallas kernels: none -> 241 us  [per_device(): pl.pallas_call(kernel, out_shape=(jax.ShapeDtypeStruct((rows, width), bf1...]
    all_gather x2 -> x0, waiting for transfers between devices: 183 us -> none  [the longest x1 120 us: per_device(): activated = lax.all_gather(squared(shares), 'gz', axis=0, tiled=True)]
    psum x1 -> x0, blocking collectives: 65.6 us -> none  [per_device(): segment_total = lax.psum(partial_total, ('gx', 'gy', 'gz'))]
    dot_general x2 -> x0, matrix products: 60.3 us -> none  [the longest x1 30.2 us: per_device(): jnp.dot(picked, up_weight, preferred_element_type=jnp.float32)]
  transfers between devices with their start and end apart: 4 -> 0, of which waited for: 4 -> 0; matrix products, arithmetic and copies ran while one was open for 0% -> 0% of each run, Pallas kernels for 0% -> 0%
where the time goes in v1:
time: 248 us; the launch traced here: 247 us
  Pallas kernels  241 us (97%)
  local copies, waits for them, and re-layouts  5.86 us (2%)
    pallas_call x1, Pallas kernels, per_device(): pl.pallas_call(kernel, out_shape=(jax.ShapeDtypeStruct((rows, width), bf1...  241 us

profile of v1, /device:TPU:1, one launch (start us, length us, event | category | flops | bytes accessed | tf_op | source)
XLA Modules:
  0.0 247.3 jit_solution(5021543780701026576)
XLA Ops:
  0.6 0.8 dynamic_slice.3
  1.4 1.3 reshape.11.read_ref
  2.7 0.7 broadcast_in_dim.2.own_ids_ref
  3.4 240.8 %feed_forward.1 = (bf16[128,2304]{1,0:T(8,128)(2,1)}, f32[8,128]{1,0:T(8,128)}) custom-call(bf16[128,2304]{1,0:T(8,128)(2,1)} %tok_hbm.1, bf16[2304,2304]{1,0:T(8,128)(2,1)} %up_hbm.1, bf16[2304,2304]{1,0:T(8,128)(2,1)} %down_hbm.1, bf16[1,2304]{1,0:T(2,128)(2,1)} %reshape.11.read_ref, s32[128,128]{1,0:T(8,128)} %broadcast_in_dim.2.own_ids_ref, ...), custom_call_target="tpu_custom_call" | custom-call | flops 43486543872 | bytes 21233664 | tf_op jit(solution)/shard_map/feed_forward/pallas_call | solution.py:371
  244.2 1.2 slice_bitcast_fusion
  245.3 1.9 copy.8

commit v2 on v1

v2 whole, which is shorter than its diff:
```python
import functools

import jax
import jax.numpy as jnp
from jax import lax
from jax.experimental import pallas as pl
from jax.experimental.pallas import tpu as pltpu
from jax.sharding import PartitionSpec as P

MESH = pl.DeviceIdType.MESH
SEGS = 8
PIECES = 16
CHUNK = 16
PART = 64
TILE = 768
PAIR_Z = (0, 1, 3, 2, 1, 3, 2, 0)
NEAR = 13
STAGES = (("own", 7), ("up", 0), ("pass", 1), ("sum", 2), ("act", 3), ("fwd", 4), ("back", 5), ("down", 6), ("pre", -1))
Y_FIRST = 1
LAST = max(lag for _, lag in STAGES)
PART_RING = 3


def packed(table, bits):
    return sum(v << (bits * k) for k, v in enumerate(table))


def lookup(table, bits, k):
    return (packed(table, bits) >> (bits * k)) % (1 << bits)


def kernel(
    tok_hbm, up_hbm, down_hbm, read_ref, ids_ref, out_ref, score_ref,
    wu, wd, tk, pf, s1s, s2s, s1r, s2r, s3s, y1s, keep, s3r, mo, acc, xs, xr, p4s, p4r, lane_sum, own_score, ar1, ar2,
    w_sem, tok_sem, p1_s, p1_r, fw_s, fw_r, s1_s, s1_r, s2_s, s2_r, s3_s, s3_r, s4_s, s4_r, s5_s, s5_r, s6_s, s6_r, s7_s, s7_r,
    x_s, x_r, p4_s, p4_r, ar1_s, ar1_r, ar2_s, ar2_r,
):
    z = lax.axis_index("gx")
    gy = lax.axis_index("gy")
    gz = lax.axis_index("gz")
    low, core = gy // 2, gy % 2
    high, x = gz // 4, gz % 4
    block = z * 4 + gy

    def in_group(gz_to):
        return (z, gy, gz_to)

    right = in_group(high * 4 + (x + 1) % 4)
    left = in_group(high * 4 + (x + 3) % 4)
    across = in_group((1 - high) * 4 + x)
    twin = (z, low * 2 + 1 - core, gz)

    def chunk(dx, j):
        at = ((x + dx) % 4) * 2 + (high + j) % 2
        return pl.ds(pl.multiple_of(at * CHUNK, CHUNK), CHUNK)

    def rcopy(src, dst, ss, rs, to):
        return pltpu.make_async_remote_copy(
            src_ref=src, dst_ref=dst, send_sem=ss, recv_sem=rs, device_id=to, device_id_type=MESH
        )

    barrier = pltpu.get_barrier_semaphore()
    for d in range(1, 8):
        pl.semaphore_signal(barrier, inc=1, device_id=in_group((gz + d) % 8), device_id_type=MESH)
    for d in range(1, 16):
        to = (block + d) % 16
        pl.semaphore_signal(barrier, inc=1, device_id=(to // 4, to % 4, gz), device_id_type=MESH)

    load_tok = pltpu.make_async_copy(tok_hbm, tk.at[0], tok_sem)
    load_down = pltpu.make_async_copy(down_hbm, wd, w_sem.at[0])

    def load_up(n):
        cols = pl.ds(pl.multiple_of(n * TILE, TILE), TILE)
        return pltpu.make_async_copy(up_hbm.at[:, cols], wu.at[:, cols], w_sem.at[n + 1])

    load_tok.start()
    for n in range(wu.shape[1] // TILE):
        load_up(n).start()
    pl.semaphore_wait(barrier, 22)

    def along(step):
        return ((z + step) % 4, gy, gz)

    beside = (z, (1 - low) * 2 + core, gz)

    def rows_of(part):
        return pl.ds(part * PART if isinstance(part, int) else pl.multiple_of(part * PART, PART), PART)

    mine, others = rows_of(0), rows_of(1)

    def gather(k, part):
        to, i = along(4 - lookup(PAIR_Z, 2, k)), 2 * k - 1 + part
        return rcopy(tok_hbm.at[rows_of(part)], tk.at[i, mine], p1_s.at[part, k], p1_r.at[i], to)

    def gather_near(k, part):
        to, i = along(4 - lookup(PAIR_Z, 2, k)), 2 * k - 1 + part
        return rcopy(tk.at[NEAR + part, mine], tk.at[i, mine], p1_s.at[part, k], p1_r.at[i], to)

    def to_near(part):
        i = NEAR + part
        return rcopy(tok_hbm.at[rows_of(part)], tk.at[i, mine], p1_s.at[part, 7], p1_r.at[i], beside)

    to_twin = rcopy(tok_hbm, tk.at[15], p1_s.at[0, 0], p1_r.at[15], twin)
    gather(1, 0).start()
    gather(2, 0).start()
    to_near(0).start()
    load_tok.wait()

    def forward(i):
        return rcopy(tk.at[i, mine], tk.at[i, others], fw_s, fw_r.at[i], twin)

    half = up_hbm.shape[1] // 2
    halves = (pl.ds(0, half), pl.ds(half, half))

    def first(i, n):
        q = i % 3
        if n < 2:
            return rcopy(s1s.at[q, n], s1r.at[i, n], s1_s.at[n, q], s1_r.at[n, i], (right, left)[n])
        return rcopy(s1s.at[q, n], s2r.at[i, n - 2], s1_s.at[n, q], s2_r.at[n - 2, i], (right, left)[n - 2])

    def second(i, n):
        q = i % 3
        return rcopy(s2s.at[q, n], s2r.at[i, n + 2], s2_s.at[n, q], s2_r.at[n + 2, i], (right, left)[n])

    def third(i):
        q = i % 3
        return rcopy(s3s.at[q], s3r.at[i], s3_s.at[q], s3_r.at[i], across)

    def y_first(i):
        return rcopy(y1s, s2r.at[i], s3_s.at[Y_FIRST], s3_r.at[i], across)

    def y_second(i, n):
        cols, to = halves[(0, 1, 1, 0)[n]], (right, left)[n % 2]
        dst = s3r.at[i, :, cols] if n < 2 else s1r.at[i, n - 2, :, cols]
        recv = s1_r.at[n, i] if n < 2 else s2_r.at[n - 2, i]
        return rcopy(s1s.at[Y_FIRST, (0, 0, 1, 2)[n], :, cols], dst, s1_s.at[n, Y_FIRST], recv, to)

    def y_third(i, n):
        src, dst = s1s.at[Y_FIRST, n + 1, :, halves[n]], s1r.at[i, n, :, halves[n]]
        return rcopy(src, dst, s2_s.at[n, Y_FIRST], s2_r.at[n + 2, i], (right, left)[n])

    def spread(i, dx, j, ss, rs, to):
        place = tk.at[i, chunk(dx, j)]
        return rcopy(place, place, ss, rs, to)

    def fourth(i):
        return spread(i, 0, 0, s4_s.at[i], s4_r.at[i], across)

    def fifth(i, j, n):
        return spread(i, 0, j, s5_s.at[2 * j + n, i], s5_r.at[2 * j + n, i], (right, left)[n])

    def fifth_in(i, j, n):
        return spread(i, (3, 1)[n], j, s5_s.at[2 * j + n, i], s5_r.at[2 * j + n, i], (right, left)[n])

    def sixth(i, n):
        return spread(i, (3, 1)[n], n, s6_s.at[n, i], s6_r.at[n, i], (right, left)[n])

    def sixth_in(i, n):
        return spread(i, 2, n, s6_s.at[n, i], s6_r.at[n, i], (right, left)[n])

    def y_sixth(i, n):
        place = tk.at[i, chunk((3, 1)[n], 0), halves[n]]
        return rcopy(place, place, s6_s.at[n, i], s6_r.at[n, i], (right, left)[n])

    def y_sixth_in(i, n):
        place = tk.at[i, chunk(2, 0), halves[n]]
        return rcopy(place, place, s6_s.at[n, i], s6_r.at[n, i], (right, left)[n])

    def y_last(i, n, j=0):
        if n < 2:
            return spread(i, (3, 1)[n], j, s5_s.at[2 + n, i], s5_r.at[2 + n, i], across)
        return spread(i, 2, j, s7_s.at[i], s7_r.at[i], across)

    def exchange(i):
        return rcopy(xs.at[i % 2], xr.at[i % 2], x_s.at[i % 2], x_r.at[i], twin)

    exchange_own = rcopy(xs, xr.at[pl.ds(2, 2)], x_s.at[2], x_r.at[15], twin)

    def owner(k, part):
        src, dst = p4s.at[1 - part], p4r.at[k - 1, rows_of(part)]
        return rcopy(src, dst, p4_s.at[1 - part], p4_r.at[part, k - 1], along(lookup(PAIR_Z, 2, k)))

    def owner_near(part):
        src, dst = p4s.at[1 - part], p4r.at[6, rows_of(part)]
        return rcopy(src, dst, p4_s.at[1 - part], p4_r.at[part, 6], beside)

    def pre(i):
        @pl.when((i > 0) & (i < NEAR))
        def _():
            rcopy(tk.at[i, mine], tk.at[i, mine], p1_s.at[0, 0], p1_r.at[i], twin).wait_recv()

        @pl.when((i > 0) & (i < PIECES - 1))
        def _():
            forward(i).start()

    def up(i):
        @pl.when((i > 0) & (i < PIECES - 1))
        def _():
            forward(i).wait_recv()

        @pl.when(i == PIECES - 1)
        def _():
            to_twin.wait_recv()

        p = i % PART_RING

        @pl.loop(0, wu.shape[1] // TILE)
        def _(n):
            cols = pl.ds(pl.multiple_of(n * TILE, TILE), TILE)

            @pl.when(i == 0)
            def _():
                load_up(n).wait()

            pf[p, :, cols] = jnp.dot(tk[i], wu[:, cols], preferred_element_type=jnp.float32)

        @pl.when((i > 0) & (i < PIECES - 1))
        def _():
            forward(i).wait_send()

        @pl.when((i >= NEAR) & (i < PIECES - 1))
        def _():
            for k in (4, 5, 6):
                gather_near(k, i - NEAR).wait_send()

        q = i % 3

        @pl.when(q != Y_FIRST)
        def _():
            s1s[q, 0] = pf[p, chunk(2, 0)].astype(jnp.bfloat16)
            s1s[q, 1] = pf[p, chunk(2, 1)].astype(jnp.bfloat16)
            first(i, 0).start()
            first(i, 1).start()
            s1s[q, 2] = pf[p, chunk(1, 1)].astype(jnp.bfloat16)
            s1s[q, 3] = pf[p, chunk(3, 0)].astype(jnp.bfloat16)
            first(i, 2).start()
            first(i, 3).start()

        @pl.when(q == Y_FIRST)
        def _():
            for d in range(4):
                y1s[d] = pf[p, chunk(d, 1)].astype(jnp.bfloat16)
            y_first(i).start()

    def by_kind(plain, crossed):
        def stage(i):
            pl.when(i % 3 != Y_FIRST)(lambda: plain(i))
            pl.when(i % 3 == Y_FIRST)(lambda: crossed(i))

        return stage

    def pass_on(i):
        p, q = i % PART_RING, i % 3
        first(i, 0).wait_recv()
        s2s[q, 0] = (pf[p, chunk(1, 0)] + s1r[i, 0].astype(jnp.float32)).astype(jnp.bfloat16)
        second(i, 0).start()
        first(i, 1).wait_recv()
        s2s[q, 1] = (pf[p, chunk(3, 1)] + s1r[i, 1].astype(jnp.float32)).astype(jnp.bfloat16)
        second(i, 1).start()

    def y_pass_on(i):
        p = i % PART_RING
        y_first(i).wait_recv()
        for n, d in enumerate((2, 1, 3)):
            total = pf[p, chunk(d, 0)] + s2r[i, d].astype(jnp.float32)
            s1s[Y_FIRST, n] = total.astype(jnp.bfloat16)
            if n:
                pf[p, chunk(d, 0)] = total
                y_second(i, n + 1).start()
            else:
                y_second(i, 0).start()
                y_second(i, 1).start()
        keep[Y_FIRST] = pf[p, chunk(0, 0)] + s2r[i, 0].astype(jnp.float32)
        y_first(i).wait_send()

    def sum_up(i):
        p, q = i % PART_RING, i % 3
        first(i, 2).wait_recv()
        second(i, 1).wait_recv()
        s3s[q] = (
            pf[p, chunk(0, 1)] + s2r[i, 0].astype(jnp.float32) + s2r[i, 3].astype(jnp.float32)
        ).astype(jnp.bfloat16)
        third(i).start()
        first(i, 3).wait_recv()
        second(i, 0).wait_recv()
        keep[q] = pf[p, chunk(0, 0)] + s2r[i, 1].astype(jnp.float32) + s2r[i, 2].astype(jnp.float32)
        for n in range(4):
            first(i, n).wait_send()

    def y_sum_up(i):
        p = i % PART_RING
        for n in range(2):
            cols = halves[n]
            y_second(i, n).wait_recv()
            total = pf[p, chunk((1, 3)[n], 0), cols] + s3r[i, :, cols].astype(jnp.float32)
            s1s[Y_FIRST, n + 1, :, cols] = total.astype(jnp.bfloat16)
            y_third(i, n).start()

    def act(i):
        third(i).wait_recv()
        total = keep[i % 3] + s3r[i].astype(jnp.float32)
        tk[i, chunk(0, 0)] = jnp.square(jnp.maximum(total, 0.0)).astype(jnp.bfloat16)
        fifth(i, 0, 0).start()
        fifth(i, 0, 1).start()
        fourth(i).start()
        second(i, 0).wait_send()
        second(i, 1).wait_send()

    def y_act(i):
        y_second(i, 2).wait_recv()
        y_second(i, 3).wait_recv()
        y_third(i, 0).wait_recv()
        y_third(i, 1).wait_recv()
        total = keep[Y_FIRST] + s1r[i, 0].astype(jnp.float32) + s1r[i, 1].astype(jnp.float32)
        tk[i, chunk(0, 0)] = jnp.square(jnp.maximum(total, 0.0)).astype(jnp.bfloat16)
        fifth(i, 0, 0).start()
        fifth(i, 0, 1).start()
        fourth(i).start()
        for n in range(4):
            y_second(i, n).wait_send()
        y_third(i, 0).wait_send()
        y_third(i, 1).wait_send()

    def fwd(i):
        spread(i, 0, 1, s4_s.at[i], s4_r.at[i], across).wait_recv()
        fifth(i, 1, 0).start()
        fifth(i, 1, 1).start()
        fifth_in(i, 0, 0).wait_recv()
        sixth(i, 0).start()
        third(i).wait_send()

    def y_fwd(i):
        for n in range(2):
            fifth_in(i, 0, n).wait_recv()
            y_sixth(i, n).start()
            y_last(i, n).start()

    def back(i):
        fifth_in(i, 1, 1).wait_recv()
        sixth(i, 1).start()

    def y_back(i):
        y_sixth_in(i, 0).wait_recv()
        y_sixth_in(i, 1).wait_recv()
        y_last(i, 2).start()

    def hidden_in(i):
        fifth_in(i, 0, 1).wait_recv()
        fifth_in(i, 1, 0).wait_recv()
        sixth_in(i, 0).wait_recv()
        sixth_in(i, 1).wait_recv()

    def y_hidden_in(i):
        spread(i, 0, 1, s4_s.at[i], s4_r.at[i], across).wait_recv()
        for n in range(3):
            y_last(i, n, 1).wait_recv()

    def sent(i):
        fourth(i).wait_send()
        for n in range(2):
            fifth(i, 0, n).wait_send()
            fifth(i, 1, n).wait_send()
            sixth(i, n).wait_send()

    def y_sent(i):
        fourth(i).wait_send()
        for n in range(2):
            fifth(i, 0, n).wait_send()
            y_sixth(i, n).wait_send()
        for n in range(3):
            y_last(i, n).wait_send()

    def lane_groups(value, cols):
        value = value * read_ref[:, cols].astype(jnp.float32)
        total = value[:, :128]
        for g in range(1, TILE // 128):
            total = total + value[:, g * 128 : (g + 1) * 128]
        return total

    def add_score(i, k):
        far = ((k >= 4) & (k < 8)).astype(jnp.int32)
        at = ((z + lookup(PAIR_Z, 2, k)) % 4) * 4 + ((low + far) % 2) * 2
        whole = (i == 0) | (i == PIECES - 1)
        upper = jnp.where(i == PIECES - 1, 1 - core, core)
        lower = jnp.where(i == 0, core, 1 - core)
        shape = lane_sum.shape
        row = lax.broadcasted_iota(jnp.int32, shape, 0)
        lane = lax.broadcasted_iota(jnp.int32, shape, 1)
        shift = jnp.where(whole, 0, jnp.where(row < PART, (1 - i % 2) * PART, (1 - i % 2) * PART - PART))
        names = jnp.where(
            row < PART,
            jnp.broadcast_to(ids_ref[pl.ds(at + upper, 1)], shape),
            jnp.broadcast_to(ids_ref[pl.ds(at + lower, 1)], shape),
        )
        row_ids = jnp.sum(jnp.where(lane == row + shift, names, 0), axis=1, keepdims=True)
        score = jnp.sum(lane_sum[...], axis=1, keepdims=True)
        part = jnp.sum(jnp.where(row_ids == lane, score, 0.0), axis=0, keepdims=True)
        own_score[0:1] = own_score[0:1] + part

    def down(i):
        @pl.when(i == 0)
        def _():
            load_down.wait()

        by_kind(hidden_in, y_hidden_in)(i)
        k = (i + 1) // 2
        lane_sum[...] = jnp.zeros_like(lane_sum)

        def product(store):
            @pl.loop(0, wd.shape[1] // TILE)
            def _(n):
                cols = pl.ds(pl.multiple_of(n * TILE, TILE), TILE)
                value = jnp.dot(tk[i], wd[:, cols], preferred_element_type=jnp.float32)
                store(cols, value)
                lane_sum[...] += lane_groups(value, cols)

        @pl.when(i == 0)
        def _():
            def store(cols, value):
                tokens = out_ref[:, cols].astype(jnp.float32)
                acc[:, cols] = value + tokens
                lane_sum[...] += lane_groups(tokens, cols)

            product(store)

        @pl.when((i > 0) & (i < PIECES - 1))
        def _():
            @pl.when(i > 2)
            def _():
                exchange(i - 2).wait_send()

            def store(cols, value):
                mo[i % 2, :, cols] = value[:PART]
                xs[i % 2, :, cols] = value[PART:]

            product(store)
            exchange(i).start()

        @pl.when(i == PIECES - 1)
        def _():
            exchange(i - 2).wait_send()
            exchange(i - 1).wait_send()

            def store(cols, value):
                xs[0, :, cols] = value[:PART]
                xs[1, :, cols] = value[PART:]

            product(store)
            exchange_own.start()

        add_score(i, k)

    def own(i):
        k, part = (i + 1) // 2, 1 - i % 2

        @pl.when((i > 0) & (i < NEAR))
        def _():
            exchange(i).wait_recv()

            @pl.when(i > 2)
            def _():
                owner(k - 1, part).wait_send()

            p4s[i % 2] = (mo[i % 2] + xr[i % 2]).astype(jnp.bfloat16)
            owner(k, part).start()

        @pl.when((i >= NEAR) & (i < PIECES - 1))
        def _():
            exchange(i).wait_recv()
            owner(6, part).wait_send()
            total = mo[i % 2] + xr[i % 2]
            rows = rows_of(part)
            for d in (4, 5, 6):
                owner(d, part).wait_recv()
                total = total + p4r[d - 1, rows].astype(jnp.float32)
            p4s[i % 2] = total.astype(jnp.bfloat16)
            owner_near(part).start()

        by_kind(sent, y_sent)(i)

    work = {
        "pre": pre,
        "up": up,
        "pass": by_kind(pass_on, y_pass_on),
        "sum": by_kind(sum_up, y_sum_up),
        "act": by_kind(act, y_act),
        "fwd": by_kind(fwd, y_fwd),
        "back": by_kind(back, y_back),
        "down": down,
        "own": own,
    }
    out_ref[...] = tk[0]
    own_score[...] = jnp.zeros_like(own_score)

    @pl.loop(0, PIECES + LAST)
    def _(t):
        @pl.when(t == 1)
        def _():
            to_twin.start()

        @pl.when(t == 2)
        def _():
            gather(3, 0).start()
            gather(3, 1).start()

        @pl.when(t == 4)
        def _():
            to_near(0).wait_recv()
            to_near(1).wait_recv()

        k = t // 2 + 2

        @pl.when((t % 2 == 0) & (k > 3) & (k < 7))
        def _():
            gather_near(k, 0).start()
            gather_near(k, 1).start()

        for name, lag in STAGES:
            @pl.when((t >= lag) & (t < lag + PIECES))
            def _(name=name, lag=lag):
                work[name](t - lag)

            if name == "up":

                @pl.when(t == 0)
                def _():
                    gather(1, 1).start()
                    gather(2, 1).start()
                    to_near(1).start()
                    load_down.start()


    ar1[gz] = own_score[...]
    in_sends = []
    for d in range(1, 8):
        in_sends.append(rcopy(ar1.at[gz], ar1.at[gz], ar1_s.at[d], ar1_r.at[d], in_group((gz + d) % 8)))
    for s in in_sends:
        s.start()
    to_twin.wait_send()
    for part in range(2):
        for k in (1, 2, 3):
            gather(k, part).wait_send()
        to_near(part).wait_send()
    for s in in_sends:
        s.wait()
    part = ar1[0]
    for d in range(1, 8):
        part = part + ar1[d]
    ar2[block] = part
    out_sends = []
    for d in range(1, 16):
        to = (block + d) % 16
        out_sends.append(rcopy(ar2.at[block], ar2.at[block], ar2_s.at[d], ar2_r.at[d], (to // 4, to % 4, gz)))
    for s in out_sends:
        s.start()

    for part in range(2):
        for k in (1, 2, 3):
            owner(k, part).wait_recv()
    exchange_own.wait_recv()
    owner_near(0).wait_recv()
    owner_near(1).wait_recv()

    @pl.loop(0, PIECES // 2)
    def _(r):
        rows = pl.ds(pl.multiple_of(r * CHUNK, CHUNK), CHUNK)
        at = pl.ds(pl.multiple_of(r % 4 * CHUNK, CHUNK), CHUNK)
        total = acc[rows] + xr[2 + r // 4, at]
        for k in (0, 1, 2, 6):
            total = total + p4r[k, rows].astype(jnp.float32)
        out_ref[rows] = total.astype(jnp.bfloat16)

    exchange_own.wait_send()
    owner_near(0).wait_send()
    owner_near(1).wait_send()
    for s in out_sends:
        s.wait()
    part = ar2[0]
    for d in range(1, 16):
        part = part + ar2[d]
    ids = ids_ref[...]
    lane = lax.broadcasted_iota(jnp.int32, (8, 128), 1)
    counts = jnp.ones((8, 128), jnp.float32)
    for s in range(SEGS):
        counts = jnp.where(lane == s, jnp.sum((ids == s).astype(jnp.float32)), counts)
    score_ref[...] = part / jnp.sqrt(counts)


def per_device(tokens, up_weight, down_weight, readout, segment_ids):
    rows, width = tokens.shape
    hidden = up_weight.shape[1]
    bf16, f32 = jnp.bfloat16, jnp.float32
    ids = segment_ids.reshape(-1, 128)
    dma = pltpu.SemaphoreType.DMA
    vmem = pl.BlockSpec(memory_space=pltpu.VMEM)
    hbm = pl.BlockSpec(memory_space=pltpu.HBM)
    mixed, scores = pl.pallas_call(
        kernel,
        out_shape=(
            jax.ShapeDtypeStruct((rows, width), bf16),
            jax.ShapeDtypeStruct((8, 128), f32),
        ),
        in_specs=[hbm, hbm, hbm, vmem, vmem],
        out_specs=(vmem, vmem),
        scratch_shapes=[
            pltpu.VMEM(up_weight.shape, bf16),
            pltpu.VMEM(down_weight.shape, bf16),
            pltpu.VMEM((PIECES, rows, width), bf16),
            pltpu.VMEM((PART_RING, rows, hidden), f32),
            pltpu.VMEM((3, 4, CHUNK, hidden), bf16),
            pltpu.VMEM((3, 2, CHUNK, hidden), bf16),
            pltpu.VMEM((PIECES, 2, CHUNK, hidden), bf16),
            pltpu.VMEM((PIECES, 4, CHUNK, hidden), bf16),
            pltpu.VMEM((3, CHUNK, hidden), bf16),
            pltpu.VMEM((4, CHUNK, hidden), bf16),
            pltpu.VMEM((3, CHUNK, hidden), f32),
            pltpu.VMEM((PIECES, CHUNK, hidden), bf16),
            pltpu.VMEM((2, PART, width), f32),
            pltpu.VMEM((rows, width), f32),
            pltpu.VMEM((2, PART, width), f32),
            pltpu.VMEM((4, PART, width), f32),
            pltpu.VMEM((2, PART, width), bf16),
            pltpu.VMEM((7, rows, width), bf16),
            pltpu.VMEM((rows, 128), f32),
            pltpu.VMEM((8, 128), f32),
            pltpu.VMEM((8, 8, 128), f32),
            pltpu.VMEM((16, 8, 128), f32),
            dma((1 + hidden // TILE,)), dma, dma((2, 8)), dma((PIECES,)), dma, dma((PIECES,)),
            dma((4, 3)), dma((2, PIECES)),
            dma((2, 3)), dma((4, PIECES)),
            dma((3,)), dma((PIECES,)),
            dma((PIECES,)), dma((PIECES,)),
            dma((4, PIECES)), dma((4, PIECES)),
            dma((2, PIECES)), dma((2, PIECES)),
            dma((PIECES,)), dma((PIECES,)),
            dma((3,)), dma((PIECES,)),
            dma((2,)), dma((2, 7)),
            dma((8,)), dma((8,)), dma((16,)), dma((16,)),
        ],
        compiler_params=pltpu.CompilerParams(
            collective_id=0, has_side_effects=True, vmem_limit_bytes=63 * 2**20
        ),
        cost_estimate=pl.CostEstimate(
            flops=4 * PIECES * rows * width * hidden, bytes_accessed=4 * width * hidden, transcendentals=0
        ),
        name="feed_forward",
    )(tokens, up_weight, down_weight, readout.reshape(1, -1), ids)
    return mixed, scores[0, :SEGS]


def solution(mesh):
    placed = (P(("gx", "gy"), "gz"), P("gz", ("gx", "gy")), P(("gx", "gy"), "gz"), P("gz"), P())
    return jax.shard_map(
        per_device,
        mesh=mesh,
        in_specs=placed,
        out_specs=(P(("gx", "gy"), "gz"), P()),
        check_vma=False,
    )
```

time: 248 us -> 199 us (0.80)
  Pallas kernels: 241 us -> 194 us
    pallas_call x1, Pallas kernels: 241 us -> 194 us  [per_device(): pl.pallas_call(kernel, out_shape=(jax.ShapeDtypeStruct((rows, width), bf1...]
where the time goes in v2:
time: 199 us
  Pallas kernels  194 us (97%)
  local copies, waits for them, and re-layouts  4.4 us (2%)
    pallas_call x1, Pallas kernels, per_device(): pl.pallas_call(kernel, out_shape=(jax.ShapeDtypeStruct((rows, width), bf1...  194 us

profile of v2, /device:TPU:1, one launch (start us, length us, event | category | flops | bytes accessed | tf_op | source)
XLA Modules:
  0.0 198.6 jit_solution(7725828068119556253)
XLA Ops:
  0.6 1.3 reshape.10.read_ref
  1.9 193.6 %feed_forward.1 = (bf16[128,2304]{1,0:T(8,128)(2,1)}, f32[8,128]{1,0:T(8,128)}) custom-call(bf16[128,2304]{1,0:T(8,128)(2,1)} %tok_hbm.1, bf16[2304,2304]{1,0:T(8,128)(2,1)} %up_hbm.1, bf16[2304,2304]{1,0:T(8,128)(2,1)} %down_hbm.1, bf16[1,2304]{1,0:T(2,128)(2,1)} %reshape.10.read_ref, s32[16,128]{1,0:T(8,128)} %bitcast.3), custom_call_target="tpu_custom_call" | custom-call | flops 43486543872 | bytes 21233664 | tf_op jit(solution)/shard_map/feed_forward/pallas_call | solution.py:597
  195.5 1.2 slice_bitcast_fusion
  196.7 1.9 copy.8

commit v3 on v2

--- a/solution.py
+++ b/solution.py
@@ -31,7 +31,7 @@
 
 def kernel(
     tok_hbm, up_hbm, down_hbm, read_ref, ids_ref, out_ref, score_ref,
-    wu, wd, tk, pf, s1s, s2s, s1r, s2r, s3s, y1s, keep, s3r, mo, acc, xs, xr, p4s, p4r, lane_sum, own_score, ar1, ar2,
+    wu, wd, tk, pf, s1s, s2s, s1r, s2r, s3s, y1s, keep, s3r, mo, acc, xs, xr, p4s, p4r, read_row, lane_sum, own_score, ar1, ar2,
     w_sem, tok_sem, p1_s, p1_r, fw_s, fw_r, s1_s, s1_r, s2_s, s2_r, s3_s, s3_r, s4_s, s4_r, s5_s, s5_r, s6_s, s6_r, s7_s, s7_r,
     x_s, x_r, p4_s, p4_r, ar1_s, ar1_r, ar2_s, ar2_r,
 ):
@@ -126,18 +126,18 @@
         q = i % 3
         return rcopy(s3s.at[q], s3r.at[i], s3_s.at[q], s3_r.at[i], across)
 
-    def y_first(i):
-        return rcopy(y1s, s2r.at[i], s3_s.at[Y_FIRST], s3_r.at[i], across)
+    def y_first(i, n):
+        if n == 0:
+            return rcopy(y1s.at[0], s2r.at[i, 0], s3_s.at[Y_FIRST], s3_r.at[i], across)
+        rest = pl.ds(1, 3)
+        return rcopy(y1s.at[rest], s2r.at[i, rest], s1_s.at[2, Y_FIRST], s2_r.at[0, i], across)
 
     def y_second(i, n):
-        cols, to = halves[(0, 1, 1, 0)[n]], (right, left)[n % 2]
-        dst = s3r.at[i, :, cols] if n < 2 else s1r.at[i, n - 2, :, cols]
-        recv = s1_r.at[n, i] if n < 2 else s2_r.at[n - 2, i]
-        return rcopy(s1s.at[Y_FIRST, (0, 0, 1, 2)[n], :, cols], dst, s1_s.at[n, Y_FIRST], recv, to)
+        src, dst = s1s.at[Y_FIRST, 0, :, halves[n]], s3r.at[i, :, halves[n]]
+        return rcopy(src, dst, s1_s.at[n, Y_FIRST], s1_r.at[n, i], (right, left)[n])
 
     def y_third(i, n):
-        src, dst = s1s.at[Y_FIRST, n + 1, :, halves[n]], s1r.at[i, n, :, halves[n]]
-        return rcopy(src, dst, s2_s.at[n, Y_FIRST], s2_r.at[n + 2, i], (right, left)[n])
+        return rcopy(s1s.at[Y_FIRST, n + 1], s1r.at[i, n], s2_s.at[n, Y_FIRST], s2_r.at[n + 2, i], (right, left)[n])
 
     def spread(i, dx, j, ss, rs, to):
         place = tk.at[i, chunk(dx, j)]
@@ -238,9 +238,11 @@
 
         @pl.when(q == Y_FIRST)
         def _():
-            for d in range(4):
-                y1s[d] = pf[p, chunk(d, 1)].astype(jnp.bfloat16)
-            y_first(i).start()
+            y1s[0] = pf[p, chunk(2, 1)].astype(jnp.bfloat16)
+            y_first(i, 0).start()
+            for n, d in enumerate((1, 3, 0)):
+                y1s[n + 1] = pf[p, chunk(d, 1)].astype(jnp.bfloat16)
+            y_first(i, 1).start()
 
     def by_kind(plain, crossed):
         def stage(i):
@@ -259,19 +261,11 @@
         second(i, 1).start()
 
     def y_pass_on(i):
-        p = i % PART_RING
-        y_first(i).wait_recv()
-        for n, d in enumerate((2, 1, 3)):
-            total = pf[p, chunk(d, 0)] + s2r[i, d].astype(jnp.float32)
-            s1s[Y_FIRST, n] = total.astype(jnp.bfloat16)
-            if n:
-                pf[p, chunk(d, 0)] = total
-                y_second(i, n + 1).start()
-            else:
-                y_second(i, 0).start()
-                y_second(i, 1).start()
-        keep[Y_FIRST] = pf[p, chunk(0, 0)] + s2r[i, 0].astype(jnp.float32)
-        y_first(i).wait_send()
+        y_first(i, 0).wait_recv()
+        total = pf[i % PART_RING, chunk(2, 0)] + s2r[i, 0].astype(jnp.float32)
+        s1s[Y_FIRST, 0] = total.astype(jnp.bfloat16)
+        y_second(i, 0).start()
+        y_second(i, 1).start()
 
     def sum_up(i):
         p, q = i % PART_RING, i % 3
@@ -289,37 +283,41 @@
 
     def y_sum_up(i):
         p = i % PART_RING
+        y_first(i, 1).wait_recv()
         for n in range(2):
-            cols = halves[n]
             y_second(i, n).wait_recv()
-            total = pf[p, chunk((1, 3)[n], 0), cols] + s3r[i, :, cols].astype(jnp.float32)
-            s1s[Y_FIRST, n + 1, :, cols] = total.astype(jnp.bfloat16)
+            for h in range(2):
+                cols = halves[h]
+                total = pf[p, chunk((1, 3)[n], 0), cols] + s2r[i, n + 1, :, cols].astype(jnp.float32)
+                if h == n:
+                    total = total + s3r[i, :, cols].astype(jnp.float32)
+                s1s[Y_FIRST, n + 1, :, cols] = total.astype(jnp.bfloat16)
             y_third(i, n).start()
+        keep[Y_FIRST] = pf[p, chunk(0, 0)] + s2r[i, 3].astype(jnp.float32)
+        y_first(i, 0).wait_send()
+        y_first(i, 1).wait_send()
 
     def act(i):
         third(i).wait_recv()
         total = keep[i % 3] + s3r[i].astype(jnp.float32)
         tk[i, chunk(0, 0)] = jnp.square(jnp.maximum(total, 0.0)).astype(jnp.bfloat16)
+        fourth(i).start()
         fifth(i, 0, 0).start()
         fifth(i, 0, 1).start()
-        fourth(i).start()
         second(i, 0).wait_send()
         second(i, 1).wait_send()
 
     def y_act(i):
-        y_second(i, 2).wait_recv()
-        y_second(i, 3).wait_recv()
         y_third(i, 0).wait_recv()
         y_third(i, 1).wait_recv()
         total = keep[Y_FIRST] + s1r[i, 0].astype(jnp.float32) + s1r[i, 1].astype(jnp.float32)
         tk[i, chunk(0, 0)] = jnp.square(jnp.maximum(total, 0.0)).astype(jnp.bfloat16)
+        fourth(i).start()
         fifth(i, 0, 0).start()
         fifth(i, 0, 1).start()
-        fourth(i).start()
-        for n in range(4):
+        for n in range(2):
             y_second(i, n).wait_send()
-        y_third(i, 0).wait_send()
-        y_third(i, 1).wait_send()
+            y_third(i, n).wait_send()
 
     def fwd(i):
         spread(i, 0, 1, s4_s.at[i], s4_r.at[i], across).wait_recv()
@@ -371,7 +369,7 @@
             y_last(i, n).wait_send()
 
     def lane_groups(value, cols):
-        value = value * read_ref[:, cols].astype(jnp.float32)
+        value = value * read_row[:, cols]
         total = value[:, :128]
         for g in range(1, TILE // 128):
             total = total + value[:, g * 128 : (g + 1) * 128]
@@ -490,6 +488,7 @@
         "own": own,
     }
     out_ref[...] = tk[0]
+    read_row[...] = read_ref[...].astype(jnp.float32).reshape(1, -1)
     own_score[...] = jnp.zeros_like(own_score)
 
     @pl.loop(0, PIECES + LAST)
@@ -621,6 +620,7 @@
             pltpu.VMEM((4, PART, width), f32),
             pltpu.VMEM((2, PART, width), bf16),
             pltpu.VMEM((7, rows, width), bf16),
+            pltpu.VMEM((1, width), f32),
             pltpu.VMEM((rows, 128), f32),
             pltpu.VMEM((8, 128), f32),
             pltpu.VMEM((8, 8, 128), f32),
@@ -644,7 +644,7 @@
             flops=4 * PIECES * rows * width * hidden, bytes_accessed=4 * width * hidden, transcendentals=0
         ),
         name="feed_forward",
-    )(tokens, up_weight, down_weight, readout.reshape(1, -1), ids)
+    )(tokens, up_weight, down_weight, readout, ids)
     return mixed, scores[0, :SEGS]
 
 

time: 199 us -> 196 us (0.985)
  Pallas kernels: 194 us -> 192 us
where the time goes in v3:
time: 196 us; the launch traced here: 195 us
  Pallas kernels  192 us (98%)
  local copies, waits for them, and re-layouts  3.1 us (2%)
    pallas_call x1, Pallas kernels, per_device(): pl.pallas_call(kernel, out_shape=(jax.ShapeDtypeStruct((rows, width), bf1...  192 us

profile of v3, /device:TPU:1, one launch (start us, length us, event | category | flops | bytes accessed | tf_op | source)
XLA Modules:
  0.0 195.3 jit_solution(10749422379856510151)
XLA Ops:
  0.6 191.6 %feed_forward.1 = (bf16[128,2304]{1,0:T(8,128)(2,1)}, f32[8,128]{1,0:T(8,128)}) custom-call(bf16[128,2304]{1,0:T(8,128)(2,1)} %tok_hbm.1, bf16[2304,2304]{1,0:T(8,128)(2,1)} %up_hbm.1, bf16[2304,2304]{1,0:T(8,128)(2,1)} %down_hbm.1, bf16[2304]{0:T(1024)(128)(2,1)} %read_ref.1, s32[16,128]{1,0:T(8,128)} %bitcast.3), custom_call_target="tpu_custom_call" | custom-call | flops 43486543872 | bytes 21233664 | tf_op jit(solution)/shard_map/feed_forward/pallas_call | solution.py:596
  192.2 1.2 slice_bitcast_fusion
  193.4 1.9 copy.8

commit v4 on v3

--- a/solution.py
+++ b/solution.py
@@ -16,7 +16,7 @@
 PAIR_Z = (0, 1, 3, 2, 1, 3, 2, 0)
 NEAR = 13
 STAGES = (("own", 7), ("up", 0), ("pass", 1), ("sum", 2), ("act", 3), ("fwd", 4), ("back", 5), ("down", 6), ("pre", -1))
-Y_FIRST = 1
+Y_FIRST = 2
 LAST = max(lag for _, lag in STAGES)
 PART_RING = 3
 

time: 196 us -> 197 us (level)
  no operation moved by 1% of the time
where the time goes in v4:
time: 197 us
  Pallas kernels  193 us (98%)
  local copies, waits for them, and re-layouts  3.1 us (2%)
    pallas_call x1, Pallas kernels, per_device(): pl.pallas_call(kernel, out_shape=(jax.ShapeDtypeStruct((rows, width), bf1...  193 us

profile of v4, /device:TPU:1, one launch (start us, length us, event | category | flops | bytes accessed | tf_op | source)
XLA Modules:
  0.0 196.6 jit_solution(8664953150032528179)
XLA Ops:
  0.6 192.9 %feed_forward.1 = (bf16[128,2304]{1,0:T(8,128)(2,1)}, f32[8,128]{1,0:T(8,128)}) custom-call(bf16[128,2304]{1,0:T(8,128)(2,1)} %tok_hbm.1, bf16[2304,2304]{1,0:T(8,128)(2,1)} %up_hbm.1, bf16[2304,2304]{1,0:T(8,128)(2,1)} %down_hbm.1, bf16[2304]{0:T(1024)(128)(2,1)} %read_ref.1, s32[16,128]{1,0:T(8,128)} %bitcast.3), custom_call_target="tpu_custom_call" | custom-call | flops 43486543872 | bytes 21233664 | tf_op jit(solution)/shard_map/feed_forward/pallas_call | solution.py:596
  193.5 1.2 slice_bitcast_fusion
  194.7 1.9 copy.8
